TPU v7x, 128 devices: a whole 4x4x4 slice. The times are simulated.
128 devices in a mesh: row: 8 (over y_lo, z), col: 16 (over x, y_hi, core).
Axes of the slice: x: 4, y: 4 (y_hi: 2, y_lo: 2; y = y_hi * 2 + y_lo), z: 4, core: 2. Of those that a mesh axis runs over, the one named last changes fastest.
Arguments:
- rhs: bfloat16 [8, 16, 128, 1024], P('row', 'col'), may hold values from -6 to 6
- operators: bfloat16 [8, 16, 3, 1024, 1024], P('row', 'col'), may hold values from -0.09375 to 0.09375
- positions: int32 [128], replicated, may hold values from 0 to 131071
- start_tick: int32 [128], replicated, may hold values from 0 to 7
Outputs:
- traces: bfloat16 [8, 16, 128, 1024], P('row', 'col')
All inputs are finite; a program needn't handle non-finite values.
Results may differ from a plain program's by a relative error of at most 0.006.
Values may be sent and summed in bfloat16 or wider, within the bound.
A program may use at most 64 MiB of HBM per device.

v0:
```python
import jax
import jax.numpy as jnp
from jax import lax
from jax.sharding import PartitionSpec as P

TICKS = 8


def passed_along(block, axis, distance):
    devices = range(lax.axis_size(axis))
    route = [(i - distance, i) for i in devices if i - distance in devices]
    return lax.ppermute(block, axis, route)


def incoming(traces, sign):
    col_count = lax.axis_size("col")
    from_row = passed_along(traces, "row", sign)
    from_col = passed_along(traces, "col", sign)
    arrived = passed_along(traces, ("row", "col"), sign * (col_count + 1))
    source_col = lax.axis_index("col") - sign
    inside = jnp.logical_and(source_col >= 0, source_col < col_count)
    diagonal_in = jnp.where(inside, arrived, jnp.zeros_like(arrived))
    return (from_row, from_col, diagonal_in)


def body(rhs, operators, positions, start_tick):
    batches = rhs.shape[2]
    trace_width = rhs.shape[3]
    operator_set = operators[0, 0]
    device_flat = lax.axis_index("row") * lax.axis_size("col") + lax.axis_index("col")
    local_point = positions - device_flat * trace_width
    column_ids = lax.broadcasted_iota(jnp.int32, (batches, trace_width), 1)
    spike_mask = (local_point[:, None] == column_ids).astype(jnp.float32)
    source = rhs[0, 0].astype(jnp.float32) + 4.0 * spike_mask
    traces = jnp.zeros((batches, trace_width), jnp.bfloat16)
    turning = TICKS // 2
    for tick_index in range(TICKS):
        summed = source
        if tick_index > 0:
            sign = 1 if tick_index < turning else -1
            from_row, from_col, diagonal_in = incoming(traces, sign)
            summed = summed + jnp.dot(from_row, operator_set[0], preferred_element_type=jnp.float32)
            summed = summed + jnp.dot(from_col, operator_set[1], preferred_element_type=jnp.float32)
            summed = summed + jnp.dot(
                diagonal_in, operator_set[2], preferred_element_type=jnp.float32
            )
        running = (tick_index >= start_tick)[:, None]
        traces = jnp.where(running, summed, 0.0).astype(jnp.bfloat16)
    return traces[None, None]


def solution(mesh):
    placed = (P("row", "col", None, None), P("row", "col", None, None, None), P(), P())
    return jax.shard_map(
        body, mesh=mesh, in_specs=placed, out_specs=P("row", "col", None, None), check_vma=False
    )
```

profile of v0, /device:TPU:98, one launch (start us, length us, event | category | flops | bytes accessed | tf_op | source)
XLA Modules:
  0.0 147.7 jit_solution(3231792398319565045)
XLA Ops:
  0.0 0.7 broadcast_compare_fusion.7
  0.7 0.7 broadcast_subtract_fusion
  1.4 1.2 select_convert_fusion
  2.6 1.9 %collective-permute-start.1 = (bf16[128,1024]{1,0:T(8,128)(2,1)S(1)}, bf16[128,1024]{1,0:T(8,128)(2,1)S(1)}, u32[]{:S(2)}, u32[]{:S(2)}) collective-permute-start(bf16[128,1024]{1,0:T(8,128)(2,1)S(1)} %select_convert_fusion), channel_id=1, source_target_pairs={{0,1},{1,2},{2,3},{3,4},{4,5},{5,6},{6,7},{7,8},{8,9},{9,10},{10,1... | collective-permute-start | bytes 786440 | tf_op jit(solution)/shard_map/ppermute | solution.py:12
  4.5 4.1 %collective-permute-start.2 = (bf16[128,1024]{1,0:T(8,128)(2,1)S(1)}, bf16[128,1024]{1,0:T(8,128)(2,1)S(1)}, u32[]{:S(2)}, u32[]{:S(2)}) collective-permute-start(bf16[128,1024]{1,0:T(8,128)(2,1)S(1)} %select_convert_fusion), channel_id=1, source_target_pairs={{0,17},{1,18},{2,19},{3,20},{4,21},{5,22},{6,23},{7,24},{8,25},{9,... | collective-permute-start | bytes 786440 | tf_op jit(solution)/shard_map/ppermute | solution.py:12
  8.6 3.8 %collective-permute-start = (bf16[128,1024]{1,0:T(8,128)(2,1)S(1)}, bf16[128,1024]{1,0:T(8,128)(2,1)S(1)}, u32[]{:S(2)}, u32[]{:S(2)}) collective-permute-start(bf16[128,1024]{1,0:T(8,128)(2,1)S(1)} %select_convert_fusion), channel_id=1, source_target_pairs={{0,16},{16,32},{32,48},{48,64},{64,80},{80,96},{96,112},{1,17},{17... | collective-permute-start | bytes 786440 | tf_op jit(solution)/shard_map/ppermute | solution.py:12
  12.6 2.2 %fusion.26 = f32[128,1024]{1,0:T(8,128)S(1)} fusion(bf16[128,1024]{1,0:T(8,128)(2,1)S(1)} %collective-permute-done.1, bf16[1,1,3,1024,1024]{4,3,2,1,0:T(8,128)(2,1)} %param.5), kind=kOutput, calls=%fused_computation.26 | convolution fusion | flops 268435456 | bytes 2883584 | tf_op jit(solution)/shard_map/dot_general | solution.py:43
  14.8 2.0 %collective-permute-done.2 = bf16[128,1024]{1,0:T(8,128)(2,1)S(1)} collective-permute-done((bf16[128,1024]{1,0:T(8,128)(2,1)S(1)}, bf16[128,1024]{1,0:T(8,128)(2,1)S(1)}, u32[]{:S(2)}, u32[]{:S(2)}) %collective-permute-start.2) | collective-permute-done | bytes 262176 | tf_op jit(solution)/shard_map/ppermute | solution.py:12
  16.8 2.0 %fusion.12 = f32[128,1024]{1,0:T(8,128)S(1)} fusion(bf16[1,1,3,1024,1024]{4,3,2,1,0:T(8,128)(2,1)} %param.5, bf16[128,1024]{1,0:T(8,128)(2,1)S(1)} %collective-permute-done.2, pred[]{:T(512)S(6)} %and.6), kind=kOutput, calls=%fused_computation.12 | convolution fusion | flops 268566528 | bytes 2883585 | tf_op jit(solution)/shard_map/dot_general | solution.py:44
  18.9 5.0 %collective-permute-done = bf16[128,1024]{1,0:T(8,128)(2,1)S(1)} collective-permute-done((bf16[128,1024]{1,0:T(8,128)(2,1)S(1)}, bf16[128,1024]{1,0:T(8,128)(2,1)S(1)}, u32[]{:S(2)}, u32[]{:S(2)}) %collective-permute-start) | collective-permute-done | bytes 262176 | tf_op jit(solution)/shard_map/ppermute | solution.py:12
  23.9 0.5 fusion.144
  24.4 2.1 %collective-permute-start.5 = (bf16[128,1024]{1,0:T(8,128)(2,1)S(1)}, bf16[128,1024]{1,0:T(8,128)(2,1)S(1)}, u32[]{:S(2)}, u32[]{:S(2)}) collective-permute-start(bf16[128,1024]{1,0:T(8,128)(2,1)S(1)} %fusion.144), channel_id=1, source_target_pairs={{0,17},{1,18},{2,19},{3,20},{4,21},{5,22},{6,23},{7,24},{8,25},{9,... | collective-permute-start | bytes 786440 | tf_op jit(solution)/shard_map/ppermute | solution.py:12
  26.6 4.7 %collective-permute-start.4 = (bf16[128,1024]{1,0:T(8,128)(2,1)S(1)}, bf16[128,1024]{1,0:T(8,128)(2,1)S(1)}, u32[]{:S(2)}, u32[]{:S(2)}) collective-permute-start(bf16[128,1024]{1,0:T(8,128)(2,1)S(1)} %fusion.144), channel_id=1, source_target_pairs={{0,1},{1,2},{2,3},{3,4},{4,5},{5,6},{6,7},{7,8},{8,9},{9,10},{10,1... | collective-permute-start | bytes 786440 | tf_op jit(solution)/shard_map/ppermute | solution.py:12
  31.3 2.0 %collective-permute-start.3 = (bf16[128,1024]{1,0:T(8,128)(2,1)S(1)}, bf16[128,1024]{1,0:T(8,128)(2,1)S(1)}, u32[]{:S(2)}, u32[]{:S(2)}) collective-permute-start(bf16[128,1024]{1,0:T(8,128)(2,1)S(1)} %fusion.144), channel_id=1, source_target_pairs={{0,16},{16,32},{32,48},{48,64},{64,80},{80,96},{96,112},{1,17},{17... | collective-permute-start | bytes 786440 | tf_op jit(solution)/shard_map/ppermute | solution.py:12
  33.3 2.2 %collective-permute-done.5 = bf16[128,1024]{1,0:T(8,128)(2,1)S(1)} collective-permute-done((bf16[128,1024]{1,0:T(8,128)(2,1)S(1)}, bf16[128,1024]{1,0:T(8,128)(2,1)S(1)}, u32[]{:S(2)}, u32[]{:S(2)}) %collective-permute-start.5) | collective-permute-done | bytes 262176 | tf_op jit(solution)/shard_map/ppermute | solution.py:12
  35.9 2.6 %collective-permute-done.4 = bf16[128,1024]{1,0:T(8,128)(2,1)S(1)} collective-permute-done((bf16[128,1024]{1,0:T(8,128)(2,1)S(1)}, bf16[128,1024]{1,0:T(8,128)(2,1)S(1)}, u32[]{:S(2)}, u32[]{:S(2)}) %collective-permute-start.4) | collective-permute-done | bytes 262176 | tf_op jit(solution)/shard_map/ppermute | solution.py:12
  39.0 3.3 %collective-permute-done.3 = bf16[128,1024]{1,0:T(8,128)(2,1)S(1)} collective-permute-done((bf16[128,1024]{1,0:T(8,128)(2,1)S(1)}, bf16[128,1024]{1,0:T(8,128)(2,1)S(1)}, u32[]{:S(2)}, u32[]{:S(2)}) %collective-permute-start.3) | collective-permute-done | bytes 262176 | tf_op jit(solution)/shard_map/ppermute | solution.py:12
  42.8 4.6 %collective-permute-start.8 = (bf16[128,1024]{1,0:T(8,128)(2,1)S(1)}, bf16[128,1024]{1,0:T(8,128)(2,1)S(1)}, u32[]{:S(2)}, u32[]{:S(2)}) collective-permute-start(bf16[128,1024]{1,0:T(8,128)(2,1)S(1)} %fusion.141), channel_id=1, source_target_pairs={{0,17},{1,18},{2,19},{3,20},{4,21},{5,22},{6,23},{7,24},{8,25},{9,... | collective-permute-start | bytes 786440 | tf_op jit(solution)/shard_map/ppermute | solution.py:12
  47.4 3.8 %collective-permute-start.7 = (bf16[128,1024]{1,0:T(8,128)(2,1)S(1)}, bf16[128,1024]{1,0:T(8,128)(2,1)S(1)}, u32[]{:S(2)}, u32[]{:S(2)}) collective-permute-start(bf16[128,1024]{1,0:T(8,128)(2,1)S(1)} %fusion.141), channel_id=1, source_target_pairs={{0,1},{1,2},{2,3},{3,4},{4,5},{5,6},{6,7},{7,8},{8,9},{9,10},{10,1... | collective-permute-start | bytes 786440 | tf_op jit(solution)/shard_map/ppermute | solution.py:12
  51.3 1.9 %collective-permute-start.6 = (bf16[128,1024]{1,0:T(8,128)(2,1)S(1)}, bf16[128,1024]{1,0:T(8,128)(2,1)S(1)}, u32[]{:S(2)}, u32[]{:S(2)}) collective-permute-start(bf16[128,1024]{1,0:T(8,128)(2,1)S(1)} %fusion.141), channel_id=1, source_target_pairs={{0,16},{16,32},{32,48},{48,64},{64,80},{80,96},{96,112},{1,17},{17... | collective-permute-start | bytes 786440 | tf_op jit(solution)/shard_map/ppermute | solution.py:12
  53.2 0.6 collective-permute-done.8
  54.3 4.4 %collective-permute-done.7 = bf16[128,1024]{1,0:T(8,128)(2,1)S(1)} collective-permute-done((bf16[128,1024]{1,0:T(8,128)(2,1)S(1)}, bf16[128,1024]{1,0:T(8,128)(2,1)S(1)}, u32[]{:S(2)}, u32[]{:S(2)}) %collective-permute-start.7) | collective-permute-done | bytes 262176 | tf_op jit(solution)/shard_map/ppermute | solution.py:12
  59.1 3.1 %collective-permute-done.6 = bf16[128,1024]{1,0:T(8,128)(2,1)S(1)} collective-permute-done((bf16[128,1024]{1,0:T(8,128)(2,1)S(1)}, bf16[128,1024]{1,0:T(8,128)(2,1)S(1)}, u32[]{:S(2)}, u32[]{:S(2)}) %collective-permute-start.6) | collective-permute-done | bytes 262176 | tf_op jit(solution)/shard_map/ppermute | solution.py:12
  62.7 2.6 %collective-permute-start.10 = (bf16[128,1024]{1,0:T(8,128)(2,1)S(1)}, bf16[128,1024]{1,0:T(8,128)(2,1)S(1)}, u32[]{:S(2)}, u32[]{:S(2)}) collective-permute-start(bf16[128,1024]{1,0:T(8,128)(2,1)S(1)} %fusion.138), channel_id=1, source_target_pairs={{1,0},{2,1},{3,2},{4,3},{5,4},{6,5},{7,6},{8,7},{9,8},{10,9},{11,1... | collective-permute-start | bytes 786440 | tf_op jit(solution)/shard_map/ppermute | solution.py:12
  65.3 1.9 %collective-permute-start.11 = (bf16[128,1024]{1,0:T(8,128)(2,1)S(1)}, bf16[128,1024]{1,0:T(8,128)(2,1)S(1)}, u32[]{:S(2)}, u32[]{:S(2)}) collective-permute-start(bf16[128,1024]{1,0:T(8,128)(2,1)S(1)} %fusion.138), channel_id=1, source_target_pairs={{17,0},{18,1},{19,2},{20,3},{21,4},{22,5},{23,6},{24,7},{25,8},{26... | collective-permute-start | bytes 786440 | tf_op jit(solution)/shard_map/ppermute | solution.py:12
  67.2 1.9 %collective-permute-start.9 = (bf16[128,1024]{1,0:T(8,128)(2,1)S(1)}, bf16[128,1024]{1,0:T(8,128)(2,1)S(1)}, u32[]{:S(2)}, u32[]{:S(2)}) collective-permute-start(bf16[128,1024]{1,0:T(8,128)(2,1)S(1)} %fusion.138), channel_id=1, source_target_pairs={{16,0},{32,16},{48,32},{64,48},{80,64},{96,80},{112,96},{17,1},{33... | collective-permute-start | bytes 786440 | tf_op jit(solution)/shard_map/ppermute | solution.py:12
  69.2 2.0 %fusion.20 = f32[128,1024]{1,0:T(8,128)S(1)} fusion(bf16[128,1024]{1,0:T(8,128)(2,1)S(1)} %collective-permute-done.10, bf16[1,1,3,1024,1024]{4,3,2,1,0:T(8,128)(2,1)} %param.5), kind=kOutput, calls=%fused_computation.20 | convolution fusion | flops 268435456 | bytes 2883584 | tf_op jit(solution)/shard_map/dot_general | solution.py:43
  71.2 10.8 %collective-permute-done.11 = bf16[128,1024]{1,0:T(8,128)(2,1)S(1)} collective-permute-done((bf16[128,1024]{1,0:T(8,128)(2,1)S(1)}, bf16[128,1024]{1,0:T(8,128)(2,1)S(1)}, u32[]{:S(2)}, u32[]{:S(2)}) %collective-permute-start.11) | collective-permute-done | bytes 262176 | tf_op jit(solution)/shard_map/ppermute | solution.py:12
  82.0 2.0 %fusion.6 = f32[128,1024]{1,0:T(8,128)S(1)} fusion(bf16[1,1,3,1024,1024]{4,3,2,1,0:T(8,128)(2,1)} %param.5, bf16[128,1024]{1,0:T(8,128)(2,1)S(1)} %collective-permute-done.11, pred[]{:T(512)S(6)} %and.14), kind=kOutput, calls=%fused_computation.6 | convolution fusion | flops 268566528 | bytes 2883585 | tf_op jit(solution)/shard_map/dot_general | solution.py:44
  84.1 2.1 %fusion.135 = bf16[128,1024]{1,0:T(8,128)(2,1)S(1)} fusion(f32[128,1024]{1,0:T(8,128)S(1)} %fusion.6, f32[128,1024]{1,0:T(8,128)S(1)} %fusion.20, bf16[128,1024]{1,0:T(8,128)(2,1)S(1)} %collective-permute-done.9, bf16[1,1,3,1024,1024]{4,3,2,1,0:T(8,128)(2,1)} %param.5, bf16[1,1,128,1024]{3,2,1,0:T(8,128)(2,1)S(1)} %copy-done, ...), kind=kOutput, calls=%fused_computation.73 | convolution fusion | flops 269615104 | bytes 3932800 | tf_op jit(solution)/shard_map/dot_general | solution.py:42
  86.2 1.9 %collective-permute-start.14 = (bf16[128,1024]{1,0:T(8,128)(2,1)S(1)}, bf16[128,1024]{1,0:T(8,128)(2,1)S(1)}, u32[]{:S(2)}, u32[]{:S(2)}) collective-permute-start(bf16[128,1024]{1,0:T(8,128)(2,1)S(1)} %fusion.135), channel_id=1, source_target_pairs={{17,0},{18,1},{19,2},{20,3},{21,4},{22,5},{23,6},{24,7},{25,8},{26... | collective-permute-start | bytes 786440 | tf_op jit(solution)/shard_map/ppermute | solution.py:12
  88.1 4.0 %collective-permute-start.13 = (bf16[128,1024]{1,0:T(8,128)(2,1)S(1)}, bf16[128,1024]{1,0:T(8,128)(2,1)S(1)}, u32[]{:S(2)}, u32[]{:S(2)}) collective-permute-start(bf16[128,1024]{1,0:T(8,128)(2,1)S(1)} %fusion.135), channel_id=1, source_target_pairs={{1,0},{2,1},{3,2},{4,3},{5,4},{6,5},{7,6},{8,7},{9,8},{10,9},{11,1... | collective-permute-start | bytes 786440 | tf_op jit(solution)/shard_map/ppermute | solution.py:12
  92.1 1.9 %collective-permute-start.12 = (bf16[128,1024]{1,0:T(8,128)(2,1)S(1)}, bf16[128,1024]{1,0:T(8,128)(2,1)S(1)}, u32[]{:S(2)}, u32[]{:S(2)}) collective-permute-start(bf16[128,1024]{1,0:T(8,128)(2,1)S(1)} %fusion.135), channel_id=1, source_target_pairs={{16,0},{32,16},{48,32},{64,48},{80,64},{96,80},{112,96},{17,1},{33... | collective-permute-start | bytes 786440 | tf_op jit(solution)/shard_map/ppermute | solution.py:12
  94.0 2.7 %collective-permute-done.14 = bf16[128,1024]{1,0:T(8,128)(2,1)S(1)} collective-permute-done((bf16[128,1024]{1,0:T(8,128)(2,1)S(1)}, bf16[128,1024]{1,0:T(8,128)(2,1)S(1)}, u32[]{:S(2)}, u32[]{:S(2)}) %collective-permute-start.14) | collective-permute-done | bytes 262176 | tf_op jit(solution)/shard_map/ppermute | solution.py:12
  97.6 8.2 %collective-permute-done.12 = bf16[128,1024]{1,0:T(8,128)(2,1)S(1)} collective-permute-done((bf16[128,1024]{1,0:T(8,128)(2,1)S(1)}, bf16[128,1024]{1,0:T(8,128)(2,1)S(1)}, u32[]{:S(2)}, u32[]{:S(2)}) %collective-permute-start.12) | collective-permute-done | bytes 262176 | tf_op jit(solution)/shard_map/ppermute | solution.py:12
  105.8 0.5 fusion.132
  106.4 1.9 %collective-permute-start.17 = (bf16[128,1024]{1,0:T(8,128)(2,1)S(1)}, bf16[128,1024]{1,0:T(8,128)(2,1)S(1)}, u32[]{:S(2)}, u32[]{:S(2)}) collective-permute-start(bf16[128,1024]{1,0:T(8,128)(2,1)S(1)} %fusion.132), channel_id=1, source_target_pairs={{17,0},{18,1},{19,2},{20,3},{21,4},{22,5},{23,6},{24,7},{25,8},{26... | collective-permute-start | bytes 786440 | tf_op jit(solution)/shard_map/ppermute | solution.py:12
  108.3 1.9 %collective-permute-start.16 = (bf16[128,1024]{1,0:T(8,128)(2,1)S(1)}, bf16[128,1024]{1,0:T(8,128)(2,1)S(1)}, u32[]{:S(2)}, u32[]{:S(2)}) collective-permute-start(bf16[128,1024]{1,0:T(8,128)(2,1)S(1)} %fusion.132), channel_id=1, source_target_pairs={{1,0},{2,1},{3,2},{4,3},{5,4},{6,5},{7,6},{8,7},{9,8},{10,9},{11,1... | collective-permute-start | bytes 786440 | tf_op jit(solution)/shard_map/ppermute | solution.py:12
  110.3 1.9 %collective-permute-start.15 = (bf16[128,1024]{1,0:T(8,128)(2,1)S(1)}, bf16[128,1024]{1,0:T(8,128)(2,1)S(1)}, u32[]{:S(2)}, u32[]{:S(2)}) collective-permute-start(bf16[128,1024]{1,0:T(8,128)(2,1)S(1)} %fusion.132), channel_id=1, source_target_pairs={{16,0},{32,16},{48,32},{64,48},{80,64},{96,80},{112,96},{17,1},{33... | collective-permute-start | bytes 786440 | tf_op jit(solution)/shard_map/ppermute | solution.py:12
  112.2 6.8 %collective-permute-done.17 = bf16[128,1024]{1,0:T(8,128)(2,1)S(1)} collective-permute-done((bf16[128,1024]{1,0:T(8,128)(2,1)S(1)}, bf16[128,1024]{1,0:T(8,128)(2,1)S(1)}, u32[]{:S(2)}, u32[]{:S(2)}) %collective-permute-start.17) | collective-permute-done | bytes 262176 | tf_op jit(solution)/shard_map/ppermute | solution.py:12
  119.9 6.5 %collective-permute-done.15 = bf16[128,1024]{1,0:T(8,128)(2,1)S(1)} collective-permute-done((bf16[128,1024]{1,0:T(8,128)(2,1)S(1)}, bf16[128,1024]{1,0:T(8,128)(2,1)S(1)}, u32[]{:S(2)}, u32[]{:S(2)}) %collective-permute-start.15) | collective-permute-done | bytes 262176 | tf_op jit(solution)/shard_map/ppermute | solution.py:12
  126.5 0.6 fusion.129
  127.0 1.9 %collective-permute-start.20 = (bf16[128,1024]{1,0:T(8,128)(2,1)S(1)}, bf16[128,1024]{1,0:T(8,128)(2,1)S(1)}, u32[]{:S(2)}, u32[]{:S(2)}) collective-permute-start(bf16[128,1024]{1,0:T(8,128)(2,1)S(1)} %fusion.129), channel_id=1, source_target_pairs={{17,0},{18,1},{19,2},{20,3},{21,4},{22,5},{23,6},{24,7},{25,8},{26... | collective-permute-start | bytes 786440 | tf_op jit(solution)/shard_map/ppermute | solution.py:12
  128.9 1.9 %collective-permute-start.19 = (bf16[128,1024]{1,0:T(8,128)(2,1)S(1)}, bf16[128,1024]{1,0:T(8,128)(2,1)S(1)}, u32[]{:S(2)}, u32[]{:S(2)}) collective-permute-start(bf16[128,1024]{1,0:T(8,128)(2,1)S(1)} %fusion.129), channel_id=1, source_target_pairs={{1,0},{2,1},{3,2},{4,3},{5,4},{6,5},{7,6},{8,7},{9,8},{10,9},{11,1... | collective-permute-start | bytes 786440 | tf_op jit(solution)/shard_map/ppermute | solution.py:12
  130.9 1.9 %collective-permute-start.18 = (bf16[128,1024]{1,0:T(8,128)(2,1)S(1)}, bf16[128,1024]{1,0:T(8,128)(2,1)S(1)}, u32[]{:S(2)}, u32[]{:S(2)}) collective-permute-start(bf16[128,1024]{1,0:T(8,128)(2,1)S(1)} %fusion.129), channel_id=1, source_target_pairs={{16,0},{32,16},{48,32},{64,48},{80,64},{96,80},{112,96},{17,1},{33... | collective-permute-start | bytes 786440 | tf_op jit(solution)/shard_map/ppermute | solution.py:12
  132.8 5.9 %collective-permute-done.20 = bf16[128,1024]{1,0:T(8,128)(2,1)S(1)} collective-permute-done((bf16[128,1024]{1,0:T(8,128)(2,1)S(1)}, bf16[128,1024]{1,0:T(8,128)(2,1)S(1)}, u32[]{:S(2)}, u32[]{:S(2)}) %collective-permute-start.20) | collective-permute-done | bytes 262176 | tf_op jit(solution)/shard_map/ppermute | solution.py:12
  139.6 6.8 %collective-permute-done.18 = bf16[128,1024]{1,0:T(8,128)(2,1)S(1)} collective-permute-done((bf16[128,1024]{1,0:T(8,128)(2,1)S(1)}, bf16[128,1024]{1,0:T(8,128)(2,1)S(1)}, u32[]{:S(2)}, u32[]{:S(2)}) %collective-permute-start.18) | collective-permute-done | bytes 262176 | tf_op jit(solution)/shard_map/ppermute | solution.py:12
  146.4 1.3 fusion.147
  (27 shorter events, 5.8 us)
Async XLA Ops:
  0.0 23.9 %copy-start = (bf16[1,1,128,1024]{3,2,1,0:T(8,128)(2,1)S(1)}, bf16[1,1,128,1024]{3,2,1,0:T(8,128)(2,1)}, u32[]{:S(2)}) copy-start(bf16[1,1,128,1024]{3,2,1,0:T(8,128)(2,1)} %param.4) | copy-start | bytes 786436
  2.6 10.1 %collective-permute-start.1 = (bf16[128,1024]{1,0:T(8,128)(2,1)S(1)}, bf16[128,1024]{1,0:T(8,128)(2,1)S(1)}, u32[]{:S(2)}, u32[]{:S(2)}) collective-permute-start(bf16[128,1024]{1,0:T(8,128)(2,1)S(1)} %select_convert_fusion), channel_id=1, source_target_pairs={{0,1},{1,2},{2,3},{3,4},{4,5},{5,6},{6,7},{7,8},{8,9},{9,10},{10,1... | collective-permute-start | bytes 786440 | tf_op jit(solution)/shard_map/ppermute | solution.py:12
  4.5 12.3 %collective-permute-start.2 = (bf16[128,1024]{1,0:T(8,128)(2,1)S(1)}, bf16[128,1024]{1,0:T(8,128)(2,1)S(1)}, u32[]{:S(2)}, u32[]{:S(2)}) collective-permute-start(bf16[128,1024]{1,0:T(8,128)(2,1)S(1)} %select_convert_fusion), channel_id=1, source_target_pairs={{0,17},{1,18},{2,19},{3,20},{4,21},{5,22},{6,23},{7,24},{8,25},{9,... | collective-permute-start | bytes 786440 | tf_op jit(solution)/shard_map/ppermute | solution.py:12
  8.6 15.3 %collective-permute-start = (bf16[128,1024]{1,0:T(8,128)(2,1)S(1)}, bf16[128,1024]{1,0:T(8,128)(2,1)S(1)}, u32[]{:S(2)}, u32[]{:S(2)}) collective-permute-start(bf16[128,1024]{1,0:T(8,128)(2,1)S(1)} %select_convert_fusion), channel_id=1, source_target_pairs={{0,16},{16,32},{32,48},{48,64},{64,80},{80,96},{96,112},{1,17},{17... | collective-permute-start | bytes 786440 | tf_op jit(solution)/shard_map/ppermute | solution.py:12
  12.5 11.5 %copy-start.1 = (bf16[1,1,3,1024,1024]{4,3,2,1,0:T(8,128)(2,1)S(1)}, bf16[1,1,3,1024,1024]{4,3,2,1,0:T(8,128)(2,1)}, u32[]{:S(2)}) copy-start(bf16[1,1,3,1024,1024]{4,3,2,1,0:T(8,128)(2,1)} %param.5) | copy-start | bytes 18874372
  24.4 11.0 %collective-permute-start.5 = (bf16[128,1024]{1,0:T(8,128)(2,1)S(1)}, bf16[128,1024]{1,0:T(8,128)(2,1)S(1)}, u32[]{:S(2)}, u32[]{:S(2)}) collective-permute-start(bf16[128,1024]{1,0:T(8,128)(2,1)S(1)} %fusion.144), channel_id=1, source_target_pairs={{0,17},{1,18},{2,19},{3,20},{4,21},{5,22},{6,23},{7,24},{8,25},{9,... | collective-permute-start | bytes 786440 | tf_op jit(solution)/shard_map/ppermute | solution.py:12
  26.6 12.0 %collective-permute-start.4 = (bf16[128,1024]{1,0:T(8,128)(2,1)S(1)}, bf16[128,1024]{1,0:T(8,128)(2,1)S(1)}, u32[]{:S(2)}, u32[]{:S(2)}) collective-permute-start(bf16[128,1024]{1,0:T(8,128)(2,1)S(1)} %fusion.144), channel_id=1, source_target_pairs={{0,1},{1,2},{2,3},{3,4},{4,5},{5,6},{6,7},{7,8},{8,9},{9,10},{10,1... | collective-permute-start | bytes 786440 | tf_op jit(solution)/shard_map/ppermute | solution.py:12
  31.3 11.0 %collective-permute-start.3 = (bf16[128,1024]{1,0:T(8,128)(2,1)S(1)}, bf16[128,1024]{1,0:T(8,128)(2,1)S(1)}, u32[]{:S(2)}, u32[]{:S(2)}) collective-permute-start(bf16[128,1024]{1,0:T(8,128)(2,1)S(1)} %fusion.144), channel_id=1, source_target_pairs={{0,16},{16,32},{32,48},{48,64},{64,80},{80,96},{96,112},{1,17},{17... | collective-permute-start | bytes 786440 | tf_op jit(solution)/shard_map/ppermute | solution.py:12
  42.8 11.0 %collective-permute-start.8 = (bf16[128,1024]{1,0:T(8,128)(2,1)S(1)}, bf16[128,1024]{1,0:T(8,128)(2,1)S(1)}, u32[]{:S(2)}, u32[]{:S(2)}) collective-permute-start(bf16[128,1024]{1,0:T(8,128)(2,1)S(1)} %fusion.141), channel_id=1, source_target_pairs={{0,17},{1,18},{2,19},{3,20},{4,21},{5,22},{6,23},{7,24},{8,25},{9,... | collective-permute-start | bytes 786440 | tf_op jit(solution)/shard_map/ppermute | solution.py:12
  47.4 11.2 %collective-permute-start.7 = (bf16[128,1024]{1,0:T(8,128)(2,1)S(1)}, bf16[128,1024]{1,0:T(8,128)(2,1)S(1)}, u32[]{:S(2)}, u32[]{:S(2)}) collective-permute-start(bf16[128,1024]{1,0:T(8,128)(2,1)S(1)} %fusion.141), channel_id=1, source_target_pairs={{0,1},{1,2},{2,3},{3,4},{4,5},{5,6},{6,7},{7,8},{8,9},{9,10},{10,1... | collective-permute-start | bytes 786440 | tf_op jit(solution)/shard_map/ppermute | solution.py:12
  51.3 10.9 %collective-permute-start.6 = (bf16[128,1024]{1,0:T(8,128)(2,1)S(1)}, bf16[128,1024]{1,0:T(8,128)(2,1)S(1)}, u32[]{:S(2)}, u32[]{:S(2)}) collective-permute-start(bf16[128,1024]{1,0:T(8,128)(2,1)S(1)} %fusion.141), channel_id=1, source_target_pairs={{0,16},{16,32},{32,48},{48,64},{64,80},{80,96},{96,112},{1,17},{17... | collective-permute-start | bytes 786440 | tf_op jit(solution)/shard_map/ppermute | solution.py:12
  62.1 34.5 %slice-start = ((s8[6291456]{0:T(1024)(128)(4,1)}), s8[2097152]{0:T(1024)(128)(4,1)S(1)}, s32[]{:S(2)}) async-start(s8[6291456]{0:T(1024)(128)(4,1)} %bitcast.143), calls=%async_computation | async-start | bytes 4194304
  62.7 6.5 %collective-permute-start.10 = (bf16[128,1024]{1,0:T(8,128)(2,1)S(1)}, bf16[128,1024]{1,0:T(8,128)(2,1)S(1)}, u32[]{:S(2)}, u32[]{:S(2)}) collective-permute-start(bf16[128,1024]{1,0:T(8,128)(2,1)S(1)} %fusion.138), channel_id=1, source_target_pairs={{1,0},{2,1},{3,2},{4,3},{5,4},{6,5},{7,6},{8,7},{9,8},{10,9},{11,1... | collective-permute-start | bytes 786440 | tf_op jit(solution)/shard_map/ppermute | solution.py:12
  65.3 16.7 %collective-permute-start.11 = (bf16[128,1024]{1,0:T(8,128)(2,1)S(1)}, bf16[128,1024]{1,0:T(8,128)(2,1)S(1)}, u32[]{:S(2)}, u32[]{:S(2)}) collective-permute-start(bf16[128,1024]{1,0:T(8,128)(2,1)S(1)} %fusion.138), channel_id=1, source_target_pairs={{17,0},{18,1},{19,2},{20,3},{21,4},{22,5},{23,6},{24,7},{25,8},{26... | collective-permute-start | bytes 786440 | tf_op jit(solution)/shard_map/ppermute | solution.py:12
  67.2 16.8 %collective-permute-start.9 = (bf16[128,1024]{1,0:T(8,128)(2,1)S(1)}, bf16[128,1024]{1,0:T(8,128)(2,1)S(1)}, u32[]{:S(2)}, u32[]{:S(2)}) collective-permute-start(bf16[128,1024]{1,0:T(8,128)(2,1)S(1)} %fusion.138), channel_id=1, source_target_pairs={{16,0},{32,16},{48,32},{64,48},{80,64},{96,80},{112,96},{17,1},{33... | collective-permute-start | bytes 786440 | tf_op jit(solution)/shard_map/ppermute | solution.py:12
  71.2 25.5 %slice-start.1 = ((s8[6291456]{0:T(1024)(128)(4,1)}), s8[4194304]{0:T(1024)(128)(4,1)S(1)}, s32[]{:S(2)}) async-start(s8[6291456]{0:T(1024)(128)(4,1)} %bitcast.143), calls=%async_computation.1 | async-start | bytes 8388608
  86.2 10.5 %collective-permute-start.14 = (bf16[128,1024]{1,0:T(8,128)(2,1)S(1)}, bf16[128,1024]{1,0:T(8,128)(2,1)S(1)}, u32[]{:S(2)}, u32[]{:S(2)}) collective-permute-start(bf16[128,1024]{1,0:T(8,128)(2,1)S(1)} %fusion.135), channel_id=1, source_target_pairs={{17,0},{18,1},{19,2},{20,3},{21,4},{22,5},{23,6},{24,7},{25,8},{26... | collective-permute-start | bytes 786440 | tf_op jit(solution)/shard_map/ppermute | solution.py:12
  88.1 9.0 %collective-permute-start.13 = (bf16[128,1024]{1,0:T(8,128)(2,1)S(1)}, bf16[128,1024]{1,0:T(8,128)(2,1)S(1)}, u32[]{:S(2)}, u32[]{:S(2)}) collective-permute-start(bf16[128,1024]{1,0:T(8,128)(2,1)S(1)} %fusion.135), channel_id=1, source_target_pairs={{1,0},{2,1},{3,2},{4,3},{5,4},{6,5},{7,6},{8,7},{9,8},{10,9},{11,1... | collective-permute-start | bytes 786440 | tf_op jit(solution)/shard_map/ppermute | solution.py:12
  92.1 13.8 %collective-permute-start.12 = (bf16[128,1024]{1,0:T(8,128)(2,1)S(1)}, bf16[128,1024]{1,0:T(8,128)(2,1)S(1)}, u32[]{:S(2)}, u32[]{:S(2)}) collective-permute-start(bf16[128,1024]{1,0:T(8,128)(2,1)S(1)} %fusion.135), channel_id=1, source_target_pairs={{16,0},{32,16},{48,32},{64,48},{80,64},{96,80},{112,96},{17,1},{33... | collective-permute-start | bytes 786440 | tf_op jit(solution)/shard_map/ppermute | solution.py:12
  106.4 12.6 %collective-permute-start.17 = (bf16[128,1024]{1,0:T(8,128)(2,1)S(1)}, bf16[128,1024]{1,0:T(8,128)(2,1)S(1)}, u32[]{:S(2)}, u32[]{:S(2)}) collective-permute-start(bf16[128,1024]{1,0:T(8,128)(2,1)S(1)} %fusion.132), channel_id=1, source_target_pairs={{17,0},{18,1},{19,2},{20,3},{21,4},{22,5},{23,6},{24,7},{25,8},{26... | collective-permute-start | bytes 786440 | tf_op jit(solution)/shard_map/ppermute | solution.py:12
  108.3 11.1 %collective-permute-start.16 = (bf16[128,1024]{1,0:T(8,128)(2,1)S(1)}, bf16[128,1024]{1,0:T(8,128)(2,1)S(1)}, u32[]{:S(2)}, u32[]{:S(2)}) collective-permute-start(bf16[128,1024]{1,0:T(8,128)(2,1)S(1)} %fusion.132), channel_id=1, source_target_pairs={{1,0},{2,1},{3,2},{4,3},{5,4},{6,5},{7,6},{8,7},{9,8},{10,9},{11,1... | collective-permute-start | bytes 786440 | tf_op jit(solution)/shard_map/ppermute | solution.py:12
  110.3 16.2 %collective-permute-start.15 = (bf16[128,1024]{1,0:T(8,128)(2,1)S(1)}, bf16[128,1024]{1,0:T(8,128)(2,1)S(1)}, u32[]{:S(2)}, u32[]{:S(2)}) collective-permute-start(bf16[128,1024]{1,0:T(8,128)(2,1)S(1)} %fusion.132), channel_id=1, source_target_pairs={{16,0},{32,16},{48,32},{64,48},{80,64},{96,80},{112,96},{17,1},{33... | collective-permute-start | bytes 786440 | tf_op jit(solution)/shard_map/ppermute | solution.py:12
  127.0 11.7 %collective-permute-start.20 = (bf16[128,1024]{1,0:T(8,128)(2,1)S(1)}, bf16[128,1024]{1,0:T(8,128)(2,1)S(1)}, u32[]{:S(2)}, u32[]{:S(2)}) collective-permute-start(bf16[128,1024]{1,0:T(8,128)(2,1)S(1)} %fusion.129), channel_id=1, source_target_pairs={{17,0},{18,1},{19,2},{20,3},{21,4},{22,5},{23,6},{24,7},{25,8},{26... | collective-permute-start | bytes 786440 | tf_op jit(solution)/shard_map/ppermute | solution.py:12
  128.9 10.2 %collective-permute-start.19 = (bf16[128,1024]{1,0:T(8,128)(2,1)S(1)}, bf16[128,1024]{1,0:T(8,128)(2,1)S(1)}, u32[]{:S(2)}, u32[]{:S(2)}) collective-permute-start(bf16[128,1024]{1,0:T(8,128)(2,1)S(1)} %fusion.129), channel_id=1, source_target_pairs={{1,0},{2,1},{3,2},{4,3},{5,4},{6,5},{7,6},{8,7},{9,8},{10,9},{11,1... | collective-permute-start | bytes 786440 | tf_op jit(solution)/shard_map/ppermute | solution.py:12
  130.9 15.6 %collective-permute-start.18 = (bf16[128,1024]{1,0:T(8,128)(2,1)S(1)}, bf16[128,1024]{1,0:T(8,128)(2,1)S(1)}, u32[]{:S(2)}, u32[]{:S(2)}) collective-permute-start(bf16[128,1024]{1,0:T(8,128)(2,1)S(1)} %fusion.129), channel_id=1, source_target_pairs={{16,0},{32,16},{48,32},{64,48},{80,64},{96,80},{112,96},{17,1},{33... | collective-permute-start | bytes 786440 | tf_op jit(solution)/shard_map/ppermute | solution.py:12
where the time goes:
time: 149 us; the launch traced here: 148 us
  waiting for transfers between devices  71.1 us (48%)
  starting transfers between devices  54.8 us (37%)
  matrix products  18.9 us (13%)
  other arithmetic  2.54 us (2%)
    ppermute x21, waiting for transfers between devices, passed_along(): return lax.ppermute(block, axis, route)  71.1 us
    ppermute x21, starting transfers between devices, passed_along(): return lax.ppermute(block, axis, route)  54.8 us
    dot_general x7, matrix products, body(): jnp.dot(from_col, operator_set[1], preferred_element_type=jnp.float32)  6.48 us
    dot_general x7, matrix products, body(): jnp.dot(diagonal_in, operator_set[2], preferred_element_type=jnp.float32)  6.33 us
    dot_general x7, matrix products, body(): jnp.dot(from_row, operator_set[0], preferred_element_type=jnp.float32)  6.06 us
  transfers between devices with their start and end apart: 21, of which 16 were waited for; matrix products, arithmetic and copies ran while one was open for 9% of the time, Pallas kernels for 0%

commit v1 on v0

v1 whole, which is shorter than its diff:
```python
import functools

import jax
import jax.numpy as jnp
from jax import lax
from jax.experimental import pallas as pl
from jax.experimental.pallas import tpu as pltpu
from jax.sharding import PartitionSpec as P

TICKS = 8
TURN = 4
GROUPS = (32, 32, 32, 32)
DIRECT_ON = True
DIRECT_OFF = False
VIA = (0, 1, 2, 3)
HALF = 4
LAG = 0


def sweep_kernel(
    rhs_ref, ops_hbm, pos_ref, start_ref, out_ref,
    ops, traces, up, left, corner, via, source, start, acc,
    op_sem, up_send, up_recv, left_send, left_recv, cor_send, cor_recv,
    via_send, via_recv, pass_send,
):
    row, col = lax.axis_index("row"), lax.axis_index("col")
    rows, cols = lax.axis_size("row"), lax.axis_size("col")
    batches, width = rhs_ref.shape
    last = TICKS - 1

    def op_copy(n):
        return pltpu.make_async_copy(ops_hbm.at[n], ops.at[n], op_sem.at[n])

    for n in range(3):
        op_copy(n).start()

    def in_rows(r):
        return jnp.logical_and(r >= 0, r < rows)

    def in_cols(c):
        return jnp.logical_and(c >= 0, c < cols)

    partners = [(-1, 0), (1, 0), (0, -1), (0, 1)]
    if DIRECT_ON or DIRECT_OFF:
        partners += [(-1, -1), (1, 1)]
    slot = lax.rem(row, HALF)
    is_end = jnp.logical_or(slot == 0, slot == HALF - 1)
    other_end = jnp.where(slot == 0, row + HALF - 1, row - (HALF - 1))
    other_half = lax.rem(row + HALF, 2 * HALF)

    barrier = pltpu.get_barrier_semaphore()

    def greet(r, c):
        pl.semaphore_signal(barrier, inc=1, device_id={"row": r, "col": c})

    for dr, dc in partners:
        @pl.when(jnp.logical_and(in_rows(row + dr), in_cols(col + dc)))
        def _(dr=dr, dc=dc):
            greet(row + dr, col + dc)

    @pl.when(is_end)
    def _():
        greet(other_end, col)
        greet(other_half, col)

    pos = jnp.broadcast_to(pos_ref[...], (batches, batches)).T
    first = jnp.broadcast_to(start_ref[...], (batches, batches)).T
    start[...] = first
    own = pos - (row * cols + col) * width
    lane = lax.broadcasted_iota(jnp.int32, (batches, batches), 1)
    for c in range(width // batches):
        cut = pl.ds(c * batches, batches)
        spike = jnp.where(own == lane + c * batches, 4.0, 0.0)
        value = rhs_ref[:, cut].astype(jnp.float32) + spike
        source[:, cut] = value
        traces[1, :, cut] = jnp.where(first <= 0, value, 0.0).astype(jnp.bfloat16)

    def sign_of(k):
        return jnp.where(k < TURN, 1, -1)

    def on_chip(c, s):
        return lax.rem(c, 2) == jnp.where(s > 0, 0, 1)

    def direct(c, s):
        on = on_chip(c, s)
        return jnp.logical_or(
            jnp.logical_and(on, DIRECT_ON), jnp.logical_and(jnp.logical_not(on), DIRECT_OFF)
        )

    bounds = []
    at = 0
    for size in GROUPS:
        bounds.append((at, size))
        at += size

    def remote(src, dst, send, recv, r, c):
        return pltpu.make_async_remote_copy(
            src, dst, send, recv, device_id={"row": r, "col": c},
            device_id_type=pl.DeviceIdType.MESH,
        )

    def up_copy(k, g, s):
        a, n = bounds[g]
        return remote(traces.at[k, pl.ds(a, n)], up.at[k, pl.ds(a, n)],
                      up_send.at[k, g], up_recv.at[k, g], row + s, col)

    def left_copy(k, g, s):
        a, n = bounds[g]
        return remote(traces.at[k, pl.ds(a, n)], left.at[k, pl.ds(a, n)],
                      left_send.at[k, g], left_recv.at[k, g], row, col + s)

    def diag_copy(k, g, s):
        a, n = bounds[g]
        return remote(traces.at[k, pl.ds(a, n)], corner.at[k, pl.ds(a, n)],
                      cor_send.at[k, g], cor_recv.at[k, g], row + s, col + s)

    def relay_copy(k, g, s):
        a, n = bounds[g]
        return remote(up.at[k, pl.ds(a, n)], corner.at[k, pl.ds(a, n)],
                      cor_send.at[k, g], cor_recv.at[k, g], row, col + s)

    def via_copy(k, g, s):
        a, n = bounds[g]
        return remote(traces.at[k, pl.ds(a, n)], via.at[k, pl.ds(a, n)],
                      via_send.at[k, g], via_recv.at[k, g], other_end, col)

    def pass_copy(k, g, s):
        a, n = bounds[g]
        return remote(via.at[k, pl.ds(a, n)], up.at[k, pl.ds(a, n)],
                      pass_send.at[k, g], up_recv.at[k, g], other_half, col)

    def crosses(s):
        return row == jnp.where(s > 0, HALF - 1, HALF)

    def passes(s):
        return row == jnp.where(s > 0, 0, 2 * HALF - 1)

    def up_direct(g, s):
        to_row = in_rows(row + s)
        if g in VIA:
            to_row = jnp.logical_and(to_row, jnp.logical_not(crosses(s)))
        return to_row

    def sends(k, s):
        to_row, to_col = in_rows(row + s), in_cols(col + s)
        from_row = in_rows(row - s)
        straight = direct(col, s)
        to_diag = jnp.logical_and(jnp.logical_and(to_row, to_col), straight)
        to_relay = jnp.logical_and(jnp.logical_and(from_row, to_col), jnp.logical_not(straight))
        return to_row, to_col, to_diag, to_relay

    def send(k, g):
        s = sign_of(k)
        to_row, to_col, to_diag, _ = sends(k, s)
        pl.when(up_direct(g, s))(lambda: up_copy(k, g, s).start())
        if g in VIA:
            pl.when(crosses(s))(lambda: via_copy(k, g, s).start())
        if DIRECT_ON or DIRECT_OFF:
            pl.when(to_diag)(lambda: diag_copy(k, g, s).start())
        pl.when(to_col)(lambda: left_copy(k, g, s).start())

    peers = jnp.where(is_end, 2, 0)
    for dr, dc in partners:
        peers += jnp.where(jnp.logical_and(in_rows(row + dr), in_cols(col + dc)), 1, 0)
    pl.semaphore_wait(barrier, peers)

    for g in range(len(GROUPS)):
        send(1, g)
    for n in range(3):
        op_copy(n).wait()

    def tick(k, carry):
        s = sign_of(k)
        _, _, _, to_relay = sends(k, s)
        has_up, has_left = in_rows(row - s), in_cols(col - s)
        has_corner = jnp.logical_and(has_up, has_left)
        def straight_part(g):
            a, n = bounds[g]
            here = pl.ds(a, n)
            if g in VIA:
                @pl.when(passes(s))
                def _():
                    via_copy(k, g, s).wait_recv()
                    pass_copy(k, g, s).start()

            acc[here] = source[here]

            @pl.when(has_up)
            def _():
                up_copy(k, g, s).wait_recv()
                pl.when(to_relay)(lambda: relay_copy(k, g, s).start())
                acc[here] += jnp.dot(up[k, here], ops[0], preferred_element_type=jnp.float32)

            @pl.when(has_left)
            def _():
                left_copy(k, g, s).wait_recv()
                acc[here] += jnp.dot(left[k, here], ops[1], preferred_element_type=jnp.float32)

        def corner_part(g):
            a, n = bounds[g]
            here = pl.ds(a, n)

            @pl.when(has_corner)
            def _():
                diag_copy(k, g, s).wait_recv()
                acc[here] += jnp.dot(corner[k, here], ops[2], preferred_element_type=jnp.float32)

            for c in range(width // batches):
                cut = pl.ds(c * batches, batches)
                traces[k + 1, here, cut] = jnp.where(
                    start[here] <= k, acc[here, cut], 0.0
                ).astype(jnp.bfloat16)

            @pl.when(k < last)
            def _():
                send(k + 1, g)

        for g in range(len(GROUPS) + LAG):
            if g < len(GROUPS):
                straight_part(g)
            if g >= LAG:
                corner_part(g - LAG)
        return carry

    lax.fori_loop(1, TICKS, tick, 0)
    out_ref[...] = traces[TICKS]

    def drain(k, carry):
        s = sign_of(k)
        to_row, to_col, to_diag, to_relay = sends(k, s)
        for g in range(len(GROUPS)):
            pl.when(up_direct(g, s))(lambda: up_copy(k, g, s).wait_send())
            if g in VIA:
                pl.when(crosses(s))(lambda: via_copy(k, g, s).wait_send())
                pl.when(passes(s))(lambda: pass_copy(k, g, s).wait_send())
            pl.when(to_col)(lambda: left_copy(k, g, s).wait_send())
            pl.when(jnp.logical_or(to_diag, to_relay))(lambda: diag_copy(k, g, s).wait_send())
        return carry

    lax.fori_loop(1, TICKS, drain, 0)


def body(rhs, operators, positions, start_tick):
    batches, width = rhs.shape[2:]
    n = len(GROUPS)
    sems = pltpu.SemaphoreType.DMA((TICKS, n))
    slots = pltpu.VMEM((TICKS, batches, width), jnp.bfloat16)
    vmem = pl.BlockSpec(memory_space=pltpu.VMEM)
    out = pl.pallas_call(
        sweep_kernel,
        out_shape=jax.ShapeDtypeStruct((batches, width), jnp.bfloat16),
        in_specs=[vmem, pl.BlockSpec(memory_space=pl.ANY), vmem, vmem],
        out_specs=vmem,
        scratch_shapes=[
            pltpu.VMEM((3, width, width), jnp.bfloat16),
            pltpu.VMEM((TICKS + 1, batches, width), jnp.bfloat16),
            slots, slots, slots, slots,
            pltpu.VMEM((batches, width), jnp.float32),
            pltpu.VMEM((batches, batches), jnp.int32),
            pltpu.VMEM((batches, width), jnp.float32),
            pltpu.SemaphoreType.DMA((3,)),
            sems, sems, sems, sems, sems, sems, sems, sems, sems,
        ],
        compiler_params=pltpu.CompilerParams(
            collective_id=0, has_side_effects=True, vmem_limit_bytes=40 << 20
        ),
    )(rhs[0, 0], operators[0, 0], positions[None], start_tick[None])
    return out[None, None]


def solution(mesh):
    placed = (P("row", "col", None, None), P("row", "col", None, None, None), P(), P())
    return jax.shard_map(
        body, mesh=mesh, in_specs=placed, out_specs=P("row", "col", None, None), check_vma=False
    )
```

time: 149 us -> 84.7 us (0.57)
  the two profiles are of different devices: /device:TPU:98 before, /device:TPU:37 now
where the time goes in v1:
time: 84.7 us; the launch traced here: 84 us
  Pallas kernels  78.2 us (92%)
  local copies, waits for them, and re-layouts  5.75 us (7%)
    pallas_call x1, Pallas kernels, body(): pl.pallas_call(sweep_kernel, out_shape=jax.ShapeDtypeStruct((batches, wid...  78.2 us
    unnamed x9, local copies, waits for them, and re-layouts  5.75 us

profile of v1, /device:TPU:37, one launch (start us, length us, event | category | flops | bytes accessed | tf_op | source)
XLA Modules:
  0.0 84.0 jit_solution(14037094178991370984)
XLA Ops:
  0.0 0.0 copy-start
  0.0 2.8 %copy-done = bf16[1,1,3,1024,1024]{4,3,2,1,0:T(8,128)(2,1)S(1)} copy-done((bf16[1,1,3,1024,1024]{4,3,2,1,0:T(8,128)(2,1)S(1)}, bf16[1,1,3,1024,1024]{4,3,2,1,0:T(8,128)(2,1)}, u32[]{:S(2)}) %copy-start) | copy-done | bytes 6291480
  2.8 0.0 copy-start.1
  2.8 0.9 %copy-done.1 = bf16[1,1,128,1024]{3,2,1,0:T(8,128)(2,1)S(1)} copy-done((bf16[1,1,128,1024]{3,2,1,0:T(8,128)(2,1)S(1)}, bf16[1,1,128,1024]{3,2,1,0:T(8,128)(2,1)}, u32[]{:S(2)}) %copy-start.1) | copy-done | bytes 262168
  3.7 0.0 copy-start.2
  3.7 0.7 copy-done.2
  4.4 0.0 copy-start.3
  4.4 0.7 copy-done.3
  5.0 78.2 %shard_map.46 = bf16[128,1024]{1,0:T(8,128)(2,1)S(1)} custom-call(bf16[128,1024]{1,0:T(8,128)(2,1)S(1)} %bitcast.7, bf16[3,1024,1024]{2,1,0:T(8,128)(2,1)S(1)} %bitcast.5, s32[1,128]{1,0:T(1,128)S(1)} %bitcast.8, s32[1,128]{1,0:T(1,128)S(1)} %bitcast.9), custom_call_target="tpu_custom_call" | custom-call | tf_op jit(solution)/shard_map/pallas_call | solution.py:249
  83.3 0.7 copy.6
Async XLA Ops:
  0.0 2.8 %copy-start = (bf16[1,1,3,1024,1024]{4,3,2,1,0:T(8,128)(2,1)S(1)}, bf16[1,1,3,1024,1024]{4,3,2,1,0:T(8,128)(2,1)}, u32[]{:S(2)}) copy-start(bf16[1,1,3,1024,1024]{4,3,2,1,0:T(8,128)(2,1)} %param.5) | copy-start | bytes 18874372
  2.8 0.9 %copy-start.1 = (bf16[1,1,128,1024]{3,2,1,0:T(8,128)(2,1)S(1)}, bf16[1,1,128,1024]{3,2,1,0:T(8,128)(2,1)}, u32[]{:S(2)}) copy-start(bf16[1,1,128,1024]{3,2,1,0:T(8,128)(2,1)} %param.4) | copy-start | bytes 786436
  3.7 0.7 copy-start.2
  4.4 0.7 copy-start.3

commit v2 on v1

v2 whole, which is shorter than its diff:
```python
import functools

import jax
import jax.numpy as jnp
from jax import lax
from jax.experimental import pallas as pl
from jax.experimental.pallas import tpu as pltpu
from jax.sharding import PartitionSpec as P

TICKS = 8
TURN = 4
GROUPS = (32,)*4
DIRECT_ON = ()
DIRECT_OFF = ()
VIA = (0,1,3)
HALF = 4
ORDER = (('take', (0,)), ('late', (3,)), ('take', (1,)), ('dot', (0, 1)), ('end', (0,)), ('take', (2,)), ('end', (1,)), ('take', (3,)), ('dot', (2, 3)), ('end', (2,)))


def sweep_kernel(
    rhs_hbm, ops_hbm, pos_hbm, start_hbm, out_ref,
    rhs_ref, pos_ref, start_ref, ops, traces, up, left, corner, via, source, start, acc,
    in_sem, op_sem, up_send, up_recv, left_send, left_recv, cor_send, cor_recv,
    via_send, via_recv, pass_send, turn_send, diag_send,
):
    row, col = lax.axis_index("row"), lax.axis_index("col")
    rows, cols = lax.axis_size("row"), lax.axis_size("col")
    batches, width = rhs_hbm.shape
    last = TICKS - 1

    def op_copy(n):
        return pltpu.make_async_copy(ops_hbm.at[n], ops.at[n], op_sem.at[n])

    small = [
        pltpu.make_async_copy(there, here, in_sem.at[n])
        for n, (there, here) in enumerate(
            ((rhs_hbm, rhs_ref), (pos_hbm, pos_ref), (start_hbm, start_ref))
        )
    ]

    def in_rows(r):
        return jnp.logical_and(r >= 0, r < rows)

    def in_cols(c):
        return jnp.logical_and(c >= 0, c < cols)

    partners = [(-1, 0), (1, 0), (0, -1), (0, 1)]
    partners += [(-1, -1), (1, 1)]
    slot = lax.rem(row, HALF)
    is_end = jnp.logical_or(slot == 0, slot == HALF - 1)
    other_end = jnp.where(slot == 0, row + HALF - 1, row - (HALF - 1))
    other_half = lax.rem(row + HALF, 2 * HALF)
    beside = col + jnp.where(row < HALF, 1, -1)

    barrier = pltpu.get_barrier_semaphore()

    def greet(r, c):
        pl.semaphore_signal(barrier, inc=1, device_id={"row": r, "col": c})

    for dr, dc in partners:
        @pl.when(jnp.logical_and(in_rows(row + dr), in_cols(col + dc)))
        def _(dr=dr, dc=dc):
            greet(row + dr, col + dc)

    @pl.when(is_end)
    def _():
        greet(other_end, col)
        greet(other_half, col)

    @pl.when(jnp.logical_and(is_end, in_cols(beside)))
    def _():
        greet(other_half, beside)

    for copy in small:
        copy.start()
    for n in range(3):
        op_copy(n).start()
    for copy in small:
        copy.wait()

    pos = jnp.broadcast_to(pos_ref[...], (batches, batches)).T
    first = jnp.broadcast_to(start_ref[...], (batches, batches)).T
    start[...] = first
    own = pos - (row * cols + col) * width
    lane = lax.broadcasted_iota(jnp.int32, (batches, batches), 1)
    for c in range(width // batches):
        cut = pl.ds(c * batches, batches)
        spike = jnp.where(own == lane + c * batches, 4.0, 0.0)
        value = rhs_ref[:, cut].astype(jnp.float32) + spike
        source[:, cut] = value
        traces[1, :, cut] = jnp.where(first <= 0, value, 0.0).astype(jnp.bfloat16)

    def sign_of(k):
        return jnp.where(k < TURN, 1, -1)

    def on_chip(c, s):
        return lax.rem(c, 2) == jnp.where(s > 0, 0, 1)

    def direct(c, s, g):
        on = on_chip(c, s)
        return jnp.logical_or(
            jnp.logical_and(on, g in DIRECT_ON), jnp.logical_and(jnp.logical_not(on), g in DIRECT_OFF)
        )

    bounds = []
    at = 0
    for size in GROUPS:
        bounds.append((at, size))
        at += size

    def remote(src, dst, send, recv, r, c):
        return pltpu.make_async_remote_copy(
            src, dst, send, recv, device_id={"row": r, "col": c},
            device_id_type=pl.DeviceIdType.MESH,
        )

    def up_copy(k, g, s):
        a, n = bounds[g]
        return remote(traces.at[k, pl.ds(a, n)], up.at[k, pl.ds(a, n)],
                      up_send.at[k, g], up_recv.at[k, g], row + s, col)

    def left_copy(k, g, s):
        a, n = bounds[g]
        return remote(traces.at[k, pl.ds(a, n)], left.at[k, pl.ds(a, n)],
                      left_send.at[k, g], left_recv.at[k, g], row, col + s)

    def diag_copy(k, g, s):
        a, n = bounds[g]
        return remote(traces.at[k, pl.ds(a, n)], corner.at[k, pl.ds(a, n)],
                      diag_send.at[k, g], cor_recv.at[k, g], row + s, col + s)

    def relay_copy(k, g, s):
        a, n = bounds[g]
        return remote(up.at[k, pl.ds(a, n)], corner.at[k, pl.ds(a, n)],
                      cor_send.at[k, g], cor_recv.at[k, g], row, col + s)

    def via_copy(k, g, s):
        a, n = bounds[g]
        return remote(traces.at[k, pl.ds(a, n)], via.at[k, pl.ds(a, n)],
                      via_send.at[k, g], via_recv.at[k, g], other_end, col)

    def pass_copy(k, g, s):
        a, n = bounds[g]
        return remote(via.at[k, pl.ds(a, n)], up.at[k, pl.ds(a, n)],
                      pass_send.at[k, g], up_recv.at[k, g], other_half, col)

    def turn_copy(k, g, s):
        a, n = bounds[g]
        return remote(via.at[k, pl.ds(a, n)], corner.at[k, pl.ds(a, n)],
                      turn_send.at[k, g], cor_recv.at[k, g], other_half, col + s)

    def both(a, b):
        return jnp.logical_and(a, b)

    def crosses(s):
        return row == jnp.where(s > 0, HALF - 1, HALF)

    def enters(s):
        return row == jnp.where(s > 0, HALF, HALF - 1)

    def passes(s):
        return row == jnp.where(s > 0, 0, 2 * HALF - 1)

    def routes(g, s):
        to_row, to_col, from_row = in_rows(row + s), in_cols(col + s), in_rows(row - s)
        straight = direct(col, s, g)
        off = jnp.logical_not(on_chip(col, s))
        to_diag = straight
        if g in VIA:
            to_row_now = both(to_row, jnp.logical_not(crosses(s)))
            to_diag = both(to_diag, jnp.logical_not(both(off, crosses(s))))
        else:
            to_row_now = to_row
            to_diag = jnp.logical_or(to_diag, both(off, crosses(s)))
        bent = both(off, enters(s))
        return dict(
            up=to_row_now,
            left=to_col,
            diag=both(both(to_row, to_col), to_diag),
            relay=both(both(from_row, to_col), jnp.logical_not(jnp.logical_or(straight, bent))),
            via=crosses(s) if g in VIA else None,
            passed=passes(s) if g in VIA else None,
            turned=both(both(passes(s), to_col), off) if g in VIA else None,
        )

    def send(k, g):
        s = sign_of(k)
        route = routes(g, s)
        pl.when(route["up"])(lambda: up_copy(k, g, s).start())
        if g in VIA:
            pl.when(route["via"])(lambda: via_copy(k, g, s).start())
        pl.when(route["diag"])(lambda: diag_copy(k, g, s).start())
        pl.when(route["left"])(lambda: left_copy(k, g, s).start())

    peers = jnp.where(is_end, 2, 0) + jnp.where(jnp.logical_and(is_end, in_cols(beside)), 1, 0)
    for dr, dc in partners:
        peers += jnp.where(jnp.logical_and(in_rows(row + dr), in_cols(col + dc)), 1, 0)
    pl.semaphore_wait(barrier, peers)

    for g in range(len(GROUPS)):
        send(1, g)
    for n in range(3):
        op_copy(n).wait()

    def joined(groups):
        first, size = bounds[groups[0]][0], sum(bounds[g][1] for g in groups)
        return pl.ds(first, size)

    def pass_on(k, groups):
        s = sign_of(k)
        for g in groups:
            route = routes(g, s)
            if g in VIA:
                @pl.when(route["passed"])
                def _(g=g, route=route):
                    via_copy(k, g, s).wait_recv()
                    pl.when(route["turned"])(lambda: turn_copy(k, g, s).start())
                    pass_copy(k, g, s).start()

            @pl.when(in_rows(row - s))
            def _(g=g, route=route):
                up_copy(k, g, s).wait_recv()
                pl.when(route["relay"])(lambda: relay_copy(k, g, s).start())

    def straight_part(k, groups):
        s = sign_of(k)
        here = joined(groups)
        acc[here] = source[here]

        @pl.when(in_cols(col - s))
        def _():
            for g in groups:
                left_copy(k, g, s).wait_recv()
            acc[here] += jnp.dot(left[k, here], ops[1], preferred_element_type=jnp.float32)

        @pl.when(in_rows(row - s))
        def _():
            acc[here] += jnp.dot(up[k, here], ops[0], preferred_element_type=jnp.float32)

    def corner_part(k, groups):
        s = sign_of(k)
        here = joined(groups)

        @pl.when(jnp.logical_and(in_rows(row - s), in_cols(col - s)))
        def _():
            for g in groups:
                diag_copy(k, g, s).wait_recv()
            acc[here] += jnp.dot(corner[k, here], ops[2], preferred_element_type=jnp.float32)

        for c in range(width // batches):
            cut = pl.ds(c * batches, batches)
            traces[k + 1, here, cut] = jnp.where(
                start[here] <= k, acc[here, cut], 0.0
            ).astype(jnp.bfloat16)

        @pl.when(k < last)
        def _():
            for g in groups:
                send(k + 1, g)

    def tick(k, carry):
        for kind, groups in ORDER:
            if kind == "late":
                pl.when(k > 1)(functools.partial(corner_part, k - 1, groups))
            else:
                dict(take=pass_on, dot=straight_part, end=corner_part)[kind](k, groups)
        return carry

    lax.fori_loop(1, TICKS, tick, 0)
    for kind, groups in ORDER:
        if kind == "late":
            corner_part(last, groups)
    out_ref[...] = traces[TICKS]

    def drain(k, carry):
        s = sign_of(k)
        for g in range(len(GROUPS)):
            route = routes(g, s)
            pl.when(route["up"])(lambda: up_copy(k, g, s).wait_send())
            pl.when(route["left"])(lambda: left_copy(k, g, s).wait_send())
            pl.when(route["diag"])(lambda: diag_copy(k, g, s).wait_send())
            pl.when(route["relay"])(lambda: relay_copy(k, g, s).wait_send())
            if g in VIA:
                pl.when(route["via"])(lambda: via_copy(k, g, s).wait_send())
                pl.when(route["passed"])(lambda: pass_copy(k, g, s).wait_send())
                pl.when(route["turned"])(lambda: turn_copy(k, g, s).wait_send())
        return carry

    lax.fori_loop(1, TICKS, drain, 0)


def body(rhs, operators, positions, start_tick):
    batches, width = rhs.shape[2:]
    n = len(GROUPS)
    sems = pltpu.SemaphoreType.DMA((TICKS, n))
    slots = pltpu.VMEM((TICKS, batches, width), jnp.bfloat16)
    vmem = pl.BlockSpec(memory_space=pltpu.VMEM)
    out = pl.pallas_call(
        sweep_kernel,
        out_shape=jax.ShapeDtypeStruct((batches, width), jnp.bfloat16),
        in_specs=[pl.BlockSpec(memory_space=pltpu.HBM)] * 4,
        out_specs=vmem,
        scratch_shapes=[
            pltpu.VMEM((batches, width), jnp.bfloat16),
            pltpu.VMEM((1, batches), jnp.int32),
            pltpu.VMEM((1, batches), jnp.int32),
            pltpu.VMEM((3, width, width), jnp.bfloat16),
            pltpu.VMEM((TICKS + 1, batches, width), jnp.bfloat16),
            slots, slots, slots, slots,
            pltpu.VMEM((batches, width), jnp.float32),
            pltpu.VMEM((batches, batches), jnp.int32),
            pltpu.VMEM((batches, width), jnp.float32),
            pltpu.SemaphoreType.DMA((3,)),
            pltpu.SemaphoreType.DMA((3,)),
            sems, sems, sems, sems, sems, sems, sems, sems, sems, sems, sems,
        ],
        compiler_params=pltpu.CompilerParams(
            collective_id=0, has_side_effects=True, vmem_limit_bytes=63 << 20
        ),
    )(rhs[0, 0], operators[0, 0], positions[None], start_tick[None])
    return out[None, None]


def solution(mesh):
    placed = (P("row", "col", None, None), P("row", "col", None, None, None), P(), P())
    return jax.shard_map(
        body, mesh=mesh, in_specs=placed, out_specs=P("row", "col", None, None), check_vma=False
    )
```

time: 84.7 us -> 77.2 us (0.911)
  the two profiles are of different devices: /device:TPU:37 before, /device:TPU:33 now
where the time goes in v2:
time: 77.2 us; the launch traced here: 77 us
  Pallas kernels  75.4 us (98%)
  local copies, waits for them, and re-layouts  1.67 us (2%)
    pallas_call x1, Pallas kernels, body(): pl.pallas_call(sweep_kernel, out_shape=jax.ShapeDtypeStruct((batches, wid...  75.4 us
    unnamed x1, local copies, waits for them, and re-layouts  1.67 us

profile of v2, /device:TPU:33, one launch (start us, length us, event | category | flops | bytes accessed | tf_op | source)
XLA Modules:
  0.0 77.0 jit_solution(1271647470854529708)
XLA Ops:
  0.0 75.4 %shard_map.46 = bf16[128,1024]{1,0:T(8,128)(2,1)} custom-call(bf16[128,1024]{1,0:T(8,128)(2,1)} %bitcast.7, bf16[3,1024,1024]{2,1,0:T(8,128)(2,1)} %bitcast.5, s32[1,128]{1,0:T(1,128)} %bitcast.8, s32[1,128]{1,0:T(1,128)} %bitcast.9), custom_call_target="tpu_custom_call" | custom-call | tf_op jit(solution)/shard_map/pallas_call | solution.py:298
  75.4 1.7 %copy.6 = bf16[1,1,128,1024]{3,2,1,0:T(8,128)(2,1)} copy(bf16[1,1,128,1024]{3,2,1,0:T(8,128)(2,1)} %bitcast.6) | data formatting | bytes 524288

commit v3 on v2

--- a/solution.py
+++ b/solution.py
@@ -12,7 +12,8 @@
 GROUPS = (32,)*4
 DIRECT_ON = ()
 DIRECT_OFF = ()
-VIA = (0,1,3)
+VIA = (1,3)
+VIA_ODD = (0,1,2,3)
 HALF = 4
 ORDER = (('take', (0,)), ('late', (3,)), ('take', (1,)), ('dot', (0, 1)), ('end', (0,)), ('take', (2,)), ('end', (1,)), ('take', (3,)), ('dot', (2, 3)), ('end', (2,)))
 
@@ -166,28 +167,29 @@
         straight = direct(col, s, g)
         off = jnp.logical_not(on_chip(col, s))
         to_diag = straight
-        if g in VIA:
-            to_row_now = both(to_row, jnp.logical_not(crosses(s)))
-            to_diag = both(to_diag, jnp.logical_not(both(off, crosses(s))))
-        else:
-            to_row_now = to_row
-            to_diag = jnp.logical_or(to_diag, both(off, crosses(s)))
+        goes = jnp.where(lax.rem(col, 2) == 0, g in VIA, g in VIA_ODD)
+        leaps = both(crosses(s), goes)
+        to_row_now = both(to_row, jnp.logical_not(leaps))
+        to_diag = jnp.logical_or(
+            both(to_diag, jnp.logical_not(both(off, leaps))),
+            both(both(off, crosses(s)), jnp.logical_not(goes)),
+        )
         bent = both(off, enters(s))
         return dict(
             up=to_row_now,
             left=to_col,
             diag=both(both(to_row, to_col), to_diag),
             relay=both(both(from_row, to_col), jnp.logical_not(jnp.logical_or(straight, bent))),
-            via=crosses(s) if g in VIA else None,
-            passed=passes(s) if g in VIA else None,
-            turned=both(both(passes(s), to_col), off) if g in VIA else None,
+            via=leaps,
+            passed=both(passes(s), goes),
+            turned=both(both(both(passes(s), to_col), off), goes),
         )
 
     def send(k, g):
         s = sign_of(k)
         route = routes(g, s)
         pl.when(route["up"])(lambda: up_copy(k, g, s).start())
-        if g in VIA:
+        if g in VIA + VIA_ODD:
             pl.when(route["via"])(lambda: via_copy(k, g, s).start())
         pl.when(route["diag"])(lambda: diag_copy(k, g, s).start())
         pl.when(route["left"])(lambda: left_copy(k, g, s).start())
@@ -210,7 +212,7 @@
         s = sign_of(k)
         for g in groups:
             route = routes(g, s)
-            if g in VIA:
+            if g in VIA + VIA_ODD:
                 @pl.when(route["passed"])
                 def _(g=g, route=route):
                     via_copy(k, g, s).wait_recv()
@@ -280,7 +282,7 @@
             pl.when(route["left"])(lambda: left_copy(k, g, s).wait_send())
             pl.when(route["diag"])(lambda: diag_copy(k, g, s).wait_send())
             pl.when(route["relay"])(lambda: relay_copy(k, g, s).wait_send())
-            if g in VIA:
+            if g in VIA + VIA_ODD:
                 pl.when(route["via"])(lambda: via_copy(k, g, s).wait_send())
                 pl.when(route["passed"])(lambda: pass_copy(k, g, s).wait_send())
                 pl.when(route["turned"])(lambda: turn_copy(k, g, s).wait_send())

time: 77.2 us -> 76.7 us (level)
  the two profiles are of different devices: /device:TPU:33 before, /device:TPU:37 now
where the time goes in v3:
time: 76.7 us; the launch traced here: 76.6 us
  Pallas kernels  74.9 us (98%)
  local copies, waits for them, and re-layouts  1.67 us (2%)
    pallas_call x1, Pallas kernels, body(): pl.pallas_call(sweep_kernel, out_shape=jax.ShapeDtypeStruct((batches, wid...  74.9 us
    unnamed x1, local copies, waits for them, and re-layouts  1.67 us

profile of v3, /device:TPU:37, one launch (start us, length us, event | category | flops | bytes accessed | tf_op | source)
XLA Modules:
  0.0 76.6 jit_solution(10567706229950829156)
XLA Ops:
  0.0 74.9 %shard_map.46 = bf16[128,1024]{1,0:T(8,128)(2,1)} custom-call(bf16[128,1024]{1,0:T(8,128)(2,1)} %bitcast.7, bf16[3,1024,1024]{2,1,0:T(8,128)(2,1)} %bitcast.5, s32[1,128]{1,0:T(1,128)} %bitcast.8, s32[1,128]{1,0:T(1,128)} %bitcast.9), custom_call_target="tpu_custom_call" | custom-call | tf_op jit(solution)/shard_map/pallas_call | solution.py:300
  74.9 1.7 %copy.6 = bf16[1,1,128,1024]{3,2,1,0:T(8,128)(2,1)} copy(bf16[1,1,128,1024]{3,2,1,0:T(8,128)(2,1)} %bitcast.6) | data formatting | bytes 524288

commit v4 on v3

--- a/solution.py
+++ b/solution.py
@@ -188,11 +188,11 @@
     def send(k, g):
         s = sign_of(k)
         route = routes(g, s)
+        pl.when(route["left"])(lambda: left_copy(k, g, s).start())
         pl.when(route["up"])(lambda: up_copy(k, g, s).start())
         if g in VIA + VIA_ODD:
             pl.when(route["via"])(lambda: via_copy(k, g, s).start())
         pl.when(route["diag"])(lambda: diag_copy(k, g, s).start())
-        pl.when(route["left"])(lambda: left_copy(k, g, s).start())
 
     peers = jnp.where(is_end, 2, 0) + jnp.where(jnp.logical_and(is_end, in_cols(beside)), 1, 0)
     for dr, dc in partners:

time: 76.7 us -> 76.6 us (level)
  no operation moved by 1% of the time
where the time goes in v4:
time: 76.6 us; the launch traced here: 76.5 us
  Pallas kernels  74.8 us (98%)
  local copies, waits for them, and re-layouts  1.67 us (2%)
    pallas_call x1, Pallas kernels, body(): pl.pallas_call(sweep_kernel, out_shape=jax.ShapeDtypeStruct((batches, wid...  74.8 us
    unnamed x1, local copies, waits for them, and re-layouts  1.67 us

profile of v4, /device:TPU:37, one launch (start us, length us, event | category | flops | bytes accessed | tf_op | source)
XLA Modules:
  0.0 76.5 jit_solution(18069680625985944107)
XLA Ops:
  0.0 74.8 %shard_map.46 = bf16[128,1024]{1,0:T(8,128)(2,1)} custom-call(bf16[128,1024]{1,0:T(8,128)(2,1)} %bitcast.7, bf16[3,1024,1024]{2,1,0:T(8,128)(2,1)} %bitcast.5, s32[1,128]{1,0:T(1,128)} %bitcast.8, s32[1,128]{1,0:T(1,128)} %bitcast.9), custom_call_target="tpu_custom_call" | custom-call | tf_op jit(solution)/shard_map/pallas_call | solution.py:300
  74.8 1.7 %copy.6 = bf16[1,1,128,1024]{3,2,1,0:T(8,128)(2,1)} copy(bf16[1,1,128,1024]{3,2,1,0:T(8,128)(2,1)} %bitcast.6) | data formatting | bytes 524288
